TPU v7x, 32 devices: a whole 2x2x4 slice. The times are simulated.
32 devices in a mesh: dp: 8 (over z, x), fsdp: 4 (over y, core).
Axes of the slice: x: 2, y: 2, z: 4, core: 2. Of those that a mesh axis runs over, the one named last changes fastest.
Arguments:
- tokens: bfloat16 [3, 12288, 576], P(None, ('dp', 'fsdp')), may hold values from -6 to 6
- cotangent: bfloat16 [3, 12288, 576], P(None, ('dp', 'fsdp')), may hold values from -6 to 6
- lengths: int32 [3, 8, 3], P(None, 'dp'), may hold values from 0 to 1536, as said below
- gain_attn: bfloat16 [576], P('dp'), may hold values from 0.099609375 to 1.8984375
- w_query: bfloat16 [576, 576], P('dp', 'fsdp'), may hold values from -0.25 to 0.25
- w_key: bfloat16 [576, 192], P('dp', 'fsdp'), may hold values from -0.25 to 0.25
- w_value: bfloat16 [576, 192], P('dp', 'fsdp'), may hold values from -0.25 to 0.25
- w_out: bfloat16 [576, 576], P('dp', 'fsdp'), may hold values from -2 to 2
- gain_mlp: bfloat16 [576], P('dp'), may hold values from 0.099609375 to 1.8984375
- w_gate: bfloat16 [576, 1536], P('dp', 'fsdp'), may hold values from -0.25 to 0.25
- w_up: bfloat16 [576, 1536], P('dp', 'fsdp'), may hold values from -0.25 to 0.25
- w_down: bfloat16 [1536, 576], P('dp', 'fsdp'), may hold values from -0.15625 to 0.15625
Outputs:
- mixed: bfloat16 [3, 12288, 576], P(None, ('dp', 'fsdp'))
- input_grad: float32 [3, 12288, 576], P(None, ('dp', 'fsdp'))
- grad_gain_attn: float32 [576], P('dp')
- grad_query: float32 [576, 576], P('dp', 'fsdp')
- grad_key: float32 [576, 192], P('dp', 'fsdp')
- grad_value: float32 [576, 192], P('dp', 'fsdp')
- grad_out: float32 [576, 576], P('dp', 'fsdp')
- grad_gain_mlp: float32 [576], P('dp')
- grad_gate: float32 [576, 1536], P('dp', 'fsdp')
- grad_up: float32 [576, 1536], P('dp', 'fsdp')
- grad_down: float32 [1536, 576], P('dp', 'fsdp')
Inputs may be any that keep to these rules, and one draw needn't show every extreme that they name: lengths[m, g] lists in order the lengths of the 3 sequences (some may be empty) packed from the first token of group g of micro-batch m; they sum to at most 1536, the tokens after them being padding, and one of them is 1153 or longer.
All inputs are finite; a program needn't handle non-finite values.
Results may differ from a plain program's by a relative error of at most 0.017.
Values may be sent and summed in bfloat16 or wider, within the bound.
No kernel may reach another device: no remote copies, remote signals or barrier semaphores. Data moves between devices by JAX's collectives and lax.ppermute only.
A program may use at most 320 MiB of HBM per device.

v0:
```python
import math

import jax
import jax.numpy as jnp
from jax import lax
from jax.sharding import PartitionSpec as P

HEADS = 9
KV_HEADS = 3
HEAD_DIM = 64
FF = 1536


EPSILON = 1e-05
ROPE_BASE = 100000.0


def layout(lengths_row, token_count):
    slot_count = lengths_row.shape[0]
    ends = jnp.cumsum(lengths_row)
    starts = ends - lengths_row
    places = jnp.arange(token_count, dtype=jnp.int32)
    segment = jnp.sum((ends[None, :] <= places[:, None]).astype(jnp.int32), axis=1)
    chosen = jnp.arange(slot_count, dtype=jnp.int32)[None, :] == segment[:, None]
    begins = jnp.sum(jnp.where(chosen, starts[None, :], 0), axis=1)
    inside = segment < slot_count
    ident = jnp.where(inside, segment, slot_count + places)
    posit = jnp.where(inside, places - begins, 0)
    return (ident, posit)


def rope_tables(posit, halfway):
    freqs = jnp.exp(jnp.arange(halfway, dtype=jnp.float32) * (-math.log(ROPE_BASE) / halfway))
    angles = posit.astype(jnp.float32)[:, None] * freqs[None, :]
    return (jnp.cos(angles), jnp.sin(angles))


def rotate(vectors, cosine, sine):
    halfway = vectors.shape[-1] // 2
    first = vectors[..., :halfway]
    second = vectors[..., halfway:]
    cos_rows = cosine[:, None, :]
    sin_rows = sine[:, None, :]
    return jnp.concatenate(
        [first * cos_rows - second * sin_rows, second * cos_rows + first * sin_rows], axis=-1
    )


def unrotate(grads, cosine, sine):
    halfway = grads.shape[-1] // 2
    first = grads[..., :halfway]
    second = grads[..., halfway:]
    cos_rows = cosine[:, None, :]
    sin_rows = sine[:, None, :]
    return jnp.concatenate(
        [first * cos_rows + second * sin_rows, second * cos_rows - first * sin_rows], axis=-1
    )


def norm_back(inputs, norm_scale, gain_row, grads):
    weighted = grads * gain_row
    gain_term = jnp.sum(grads * inputs * norm_scale, axis=0)
    cubed = norm_scale * norm_scale * norm_scale
    result = norm_scale * weighted - inputs * cubed * jnp.mean(
        weighted * inputs, axis=1, keepdims=True
    )
    return (result, gain_term)


def permitted(ident_rows, posit_rows, ident_cols, posit_cols):
    return (ident_rows[:, None] == ident_cols[None, :]) & (
        posit_cols[None, :] <= posit_rows[:, None]
    )


def score_block(queries, keys_block, allowed, factor):
    raw_scores = (
        jnp.einsum("tkrd,jkd->krtj", queries, keys_block, preferred_element_type=jnp.float32)
        * factor
    )
    return jnp.where(allowed[None, None], raw_scores, -1e30)


def attend_forward(
    queries, keys_all, values_all, ident_rows, posit_rows, ident_all, posit_all, blocks, factor
):
    row_count = queries.shape[0]
    block_rows = keys_all.shape[0] // blocks
    running = jnp.full(queries.shape[1:3] + (row_count,), -1e30, jnp.float32)
    totals = jnp.zeros_like(running)
    for number in range(blocks):
        first_row = number * block_rows
        last_row = first_row + block_rows
        allowed = permitted(
            ident_rows, posit_rows, ident_all[first_row:last_row], posit_all[first_row:last_row]
        )
        scores = score_block(queries, keys_all[first_row:last_row], allowed, factor)
        updated = jnp.maximum(running, jnp.max(scores, axis=-1))
        totals = totals * jnp.exp(running - updated) + jnp.sum(
            jnp.exp(scores - updated[..., None]), axis=-1
        )
        running = updated
    logsum = running + jnp.log(totals)
    result = jnp.zeros(queries.shape, jnp.float32)
    for number in range(blocks):
        first_row = number * block_rows
        last_row = first_row + block_rows
        allowed = permitted(
            ident_rows, posit_rows, ident_all[first_row:last_row], posit_all[first_row:last_row]
        )
        scores = score_block(queries, keys_all[first_row:last_row], allowed, factor)
        probs = jnp.exp(scores - logsum[..., None]).astype(jnp.bfloat16)
        result = result + jnp.einsum(
            "krtj,jkd->tkrd",
            probs,
            values_all[first_row:last_row],
            preferred_element_type=jnp.float32,
        )
    return (logsum, result)


def attend_backward(
    queries,
    keys_all,
    values_all,
    grad_attended,
    logsum,
    ident_rows,
    posit_rows,
    ident_all,
    posit_all,
    blocks,
    factor,
):
    block_rows = keys_all.shape[0] // blocks
    row_dots = jnp.zeros_like(logsum)
    for number in range(blocks):
        first_row = number * block_rows
        last_row = first_row + block_rows
        allowed = permitted(
            ident_rows, posit_rows, ident_all[first_row:last_row], posit_all[first_row:last_row]
        )
        scores = score_block(queries, keys_all[first_row:last_row], allowed, factor)
        probs = jnp.exp(scores - logsum[..., None])
        dprobs = jnp.einsum(
            "tkrd,jkd->krtj",
            grad_attended,
            values_all[first_row:last_row],
            preferred_element_type=jnp.float32,
        )
        row_dots = row_dots + jnp.sum(dprobs * probs, axis=-1)
    grad_queries = jnp.zeros(queries.shape, jnp.float32)
    key_parts = []
    value_parts = []
    for number in range(blocks):
        first_row = number * block_rows
        last_row = first_row + block_rows
        allowed = permitted(
            ident_rows, posit_rows, ident_all[first_row:last_row], posit_all[first_row:last_row]
        )
        scores = score_block(queries, keys_all[first_row:last_row], allowed, factor)
        probs = jnp.exp(scores - logsum[..., None])
        dprobs = jnp.einsum(
            "tkrd,jkd->krtj",
            grad_attended,
            values_all[first_row:last_row],
            preferred_element_type=jnp.float32,
        )
        value_parts.append(
            jnp.einsum(
                "krtj,tkrd->jkd",
                probs.astype(jnp.bfloat16),
                grad_attended,
                preferred_element_type=jnp.float32,
            )
        )
        dscores = (probs * (dprobs - row_dots[..., None])).astype(jnp.bfloat16)
        grad_queries = grad_queries + jnp.einsum(
            "krtj,jkd->tkrd",
            dscores,
            keys_all[first_row:last_row],
            preferred_element_type=jnp.float32,
        )
        key_parts.append(
            jnp.einsum("krtj,tkrd->jkd", dscores, queries, preferred_element_type=jnp.float32)
        )
    return (
        grad_queries * factor,
        jnp.concatenate(key_parts, axis=0) * factor,
        jnp.concatenate(value_parts, axis=0),
    )


def local(
    tokens,
    cotangent,
    lengths,
    gain_attn,
    w_query,
    w_key,
    w_value,
    w_out,
    gain_mlp,
    w_gate,
    w_up,
    w_down,
):
    blocks = lax.axis_size("fsdp")
    member = lax.axis_index("fsdp")
    micro_count = tokens.shape[0]
    tok_rows = tokens.shape[1]
    width = tokens.shape[2]
    group_rows = tok_rows * blocks
    repeats = HEADS // KV_HEADS
    factor = HEAD_DIM ** (-0.5)
    halfway = HEAD_DIM // 2
    query_width = HEADS * HEAD_DIM
    kv_width = KV_HEADS * HEAD_DIM

    def fetch():
        columns = (
            lax.all_gather(w_query, "fsdp", axis=1, tiled=True),
            lax.all_gather(w_key, "fsdp", axis=1, tiled=True),
            lax.all_gather(w_value, "fsdp", axis=1, tiled=True),
            lax.all_gather(w_out, "fsdp", axis=1, tiled=True),
            lax.all_gather(w_gate, "fsdp", axis=1, tiled=True),
            lax.all_gather(w_up, "fsdp", axis=1, tiled=True),
            lax.all_gather(w_down, "fsdp", axis=1, tiled=True),
        )
        return (
            lax.all_gather(columns[0], "dp", axis=0, tiled=True),
            lax.all_gather(columns[1], "dp", axis=0, tiled=True),
            lax.all_gather(columns[2], "dp", axis=0, tiled=True),
            lax.all_gather(columns[3], "dp", axis=0, tiled=True),
            lax.all_gather(columns[4], "dp", axis=0, tiled=True),
            lax.all_gather(columns[5], "dp", axis=0, tiled=True),
            lax.all_gather(columns[6], "dp", axis=0, tiled=True),
            lax.all_gather(gain_attn, "dp", axis=0, tiled=True),
            lax.all_gather(gain_mlp, "dp", axis=0, tiled=True),
        )

    grad_query = jnp.zeros((width, query_width), jnp.float32)
    grad_key = jnp.zeros((width, kv_width), jnp.float32)
    grad_value = jnp.zeros((width, kv_width), jnp.float32)
    grad_output = jnp.zeros((query_width, width), jnp.float32)
    grad_gate = jnp.zeros((width, FF), jnp.float32)
    grad_up = jnp.zeros((width, FF), jnp.float32)
    grad_down = jnp.zeros((FF, width), jnp.float32)
    grad_gain_one = jnp.zeros((width,), jnp.float32)
    grad_gain_two = jnp.zeros((width,), jnp.float32)
    mixed_parts = []
    input_parts = []
    for number in range(micro_count):
        weights = fetch()
        gain_one = weights[7].astype(jnp.float32)
        gain_two = weights[8].astype(jnp.float32)
        inputs = tokens[number].astype(jnp.float32)
        ident_all, posit_all = layout(lengths[number, 0], group_rows)
        ident_rows = lax.dynamic_slice_in_dim(ident_all, member * tok_rows, tok_rows)
        posit_rows = lax.dynamic_slice_in_dim(posit_all, member * tok_rows, tok_rows)
        cosine, sine = rope_tables(posit_rows, halfway)
        scale_one = lax.rsqrt(jnp.mean(inputs * inputs, axis=1, keepdims=True) + EPSILON)
        normed = (inputs * scale_one * gain_one).astype(jnp.bfloat16)
        query_raw = jnp.dot(normed, weights[0], preferred_element_type=jnp.float32)
        queries = rotate(query_raw.reshape(tok_rows, HEADS, HEAD_DIM), cosine, sine).astype(
            jnp.bfloat16
        )
        key_raw = jnp.dot(normed, weights[1], preferred_element_type=jnp.float32)
        keys_rot = rotate(key_raw.reshape(tok_rows, KV_HEADS, HEAD_DIM), cosine, sine).astype(
            jnp.bfloat16
        )
        values_own = jnp.dot(normed, weights[2], preferred_element_type=jnp.float32).astype(
            jnp.bfloat16
        )
        keys_all, values_all = (
            lax.all_gather(keys_rot.reshape(tok_rows, kv_width), "fsdp", axis=0, tiled=True),
            lax.all_gather(values_own, "fsdp", axis=0, tiled=True),
        )
        keys_all = keys_all.reshape(group_rows, KV_HEADS, HEAD_DIM)
        values_all = values_all.reshape(group_rows, KV_HEADS, HEAD_DIM)
        grouped = queries.reshape(tok_rows, KV_HEADS, repeats, HEAD_DIM)
        logsum, attended = attend_forward(
            grouped,
            keys_all,
            values_all,
            ident_rows,
            posit_rows,
            ident_all,
            posit_all,
            blocks,
            factor,
        )
        attended = attended.reshape(tok_rows, query_width).astype(jnp.bfloat16)
        middle = inputs + jnp.dot(attended, weights[3], preferred_element_type=jnp.float32)
        scale_two = lax.rsqrt(jnp.mean(middle * middle, axis=1, keepdims=True) + EPSILON)
        normed_two = (middle * scale_two * gain_two).astype(jnp.bfloat16)
        gate_proj = jnp.dot(normed_two, weights[4], preferred_element_type=jnp.float32)
        up_proj = jnp.dot(normed_two, weights[5], preferred_element_type=jnp.float32)
        gate_sigmoid = jax.nn.sigmoid(gate_proj)
        hidden = (gate_proj * gate_sigmoid * up_proj).astype(jnp.bfloat16)
        mixed_parts.append(
            (middle + jnp.dot(hidden, weights[6], preferred_element_type=jnp.float32)).astype(
                jnp.bfloat16
            )
        )
        weights = fetch()
        gain_one = weights[7].astype(jnp.float32)
        gain_two = weights[8].astype(jnp.float32)
        grad_rows = cotangent[number].astype(jnp.float32)
        grad_mix = grad_rows.astype(jnp.bfloat16)
        grad_down = grad_down + jnp.einsum(
            "tf,td->fd", hidden, grad_mix, preferred_element_type=jnp.float32
        )
        grad_hidden = jnp.einsum(
            "td,fd->tf", grad_mix, weights[6], preferred_element_type=jnp.float32
        )
        grad_gate_rows = (
            grad_hidden * up_proj * gate_sigmoid * (1.0 + gate_proj * (1.0 - gate_sigmoid))
        ).astype(jnp.bfloat16)
        grad_up_rows = (grad_hidden * gate_proj * gate_sigmoid).astype(jnp.bfloat16)
        grad_gate = grad_gate + jnp.einsum(
            "tc,tf->cf", normed_two, grad_gate_rows, preferred_element_type=jnp.float32
        )
        grad_up = grad_up + jnp.einsum(
            "tc,tf->cf", normed_two, grad_up_rows, preferred_element_type=jnp.float32
        )
        grad_normed_two = jnp.einsum(
            "tf,cf->tc", grad_gate_rows, weights[4], preferred_element_type=jnp.float32
        )
        grad_normed_two = grad_normed_two + jnp.einsum(
            "tf,cf->tc", grad_up_rows, weights[5], preferred_element_type=jnp.float32
        )
        grad_middle, gain_term = norm_back(middle, scale_two, gain_two, grad_normed_two)
        grad_middle = grad_rows + grad_middle
        grad_gain_two = grad_gain_two + gain_term
        grad_branch = grad_middle.astype(jnp.bfloat16)
        grad_output = grad_output + jnp.einsum(
            "tc,td->cd", attended, grad_branch, preferred_element_type=jnp.float32
        )
        grad_attended = jnp.einsum(
            "td,cd->tc", grad_branch, weights[3], preferred_element_type=jnp.float32
        ).astype(jnp.bfloat16)
        grad_attended = grad_attended.reshape(tok_rows, KV_HEADS, repeats, HEAD_DIM)
        grad_queries, grad_keys_all, grad_values_all = attend_backward(
            grouped,
            keys_all,
            values_all,
            grad_attended,
            logsum,
            ident_rows,
            posit_rows,
            ident_all,
            posit_all,
            blocks,
            factor,
        )
        grad_keys_own, grad_values_own = (
            lax.psum_scatter(
                grad_keys_all.reshape(group_rows, kv_width).astype(jnp.bfloat16),
                "fsdp",
                scatter_dimension=0,
                tiled=True,
            ).astype(jnp.float32),
            lax.psum_scatter(
                grad_values_all.reshape(group_rows, kv_width).astype(jnp.bfloat16),
                "fsdp",
                scatter_dimension=0,
                tiled=True,
            ).astype(jnp.float32),
        )
        grad_query_rows = (
            unrotate(grad_queries.reshape(tok_rows, HEADS, HEAD_DIM), cosine, sine)
            .reshape(tok_rows, query_width)
            .astype(jnp.bfloat16)
        )
        grad_key_rows = (
            unrotate(grad_keys_own.reshape(tok_rows, KV_HEADS, HEAD_DIM), cosine, sine)
            .reshape(tok_rows, kv_width)
            .astype(jnp.bfloat16)
        )
        grad_value_rows = grad_values_own.astype(jnp.bfloat16)
        grad_query = grad_query + jnp.einsum(
            "tc,tf->cf", normed, grad_query_rows, preferred_element_type=jnp.float32
        )
        grad_key = grad_key + jnp.einsum(
            "tc,tf->cf", normed, grad_key_rows, preferred_element_type=jnp.float32
        )
        grad_value = grad_value + jnp.einsum(
            "tc,tf->cf", normed, grad_value_rows, preferred_element_type=jnp.float32
        )
        grad_normed = jnp.einsum(
            "tf,cf->tc", grad_query_rows, weights[0], preferred_element_type=jnp.float32
        )
        grad_normed = grad_normed + jnp.einsum(
            "tf,cf->tc", grad_key_rows, weights[1], preferred_element_type=jnp.float32
        )
        grad_normed = grad_normed + jnp.einsum(
            "tf,cf->tc", grad_value_rows, weights[2], preferred_element_type=jnp.float32
        )
        grad_inputs, gain_term = norm_back(inputs, scale_one, gain_one, grad_normed)
        grad_gain_one = grad_gain_one + gain_term
        input_parts.append(grad_middle + grad_inputs)
    gain_one_cols = jnp.broadcast_to(grad_gain_one[:, None], (width, blocks))
    gain_two_cols = jnp.broadcast_to(grad_gain_two[:, None], (width, blocks))
    partial_sums = (
        lax.psum_scatter(grad_query, "dp", scatter_dimension=0, tiled=True),
        lax.psum_scatter(grad_key, "dp", scatter_dimension=0, tiled=True),
        lax.psum_scatter(grad_value, "dp", scatter_dimension=0, tiled=True),
        lax.psum_scatter(grad_output, "dp", scatter_dimension=0, tiled=True),
        lax.psum_scatter(grad_gate, "dp", scatter_dimension=0, tiled=True),
        lax.psum_scatter(grad_up, "dp", scatter_dimension=0, tiled=True),
        lax.psum_scatter(grad_down, "dp", scatter_dimension=0, tiled=True),
        lax.psum_scatter(gain_one_cols, "dp", scatter_dimension=0, tiled=True),
        lax.psum_scatter(gain_two_cols, "dp", scatter_dimension=0, tiled=True),
    )
    reduced = (
        lax.psum_scatter(
            partial_sums[0].astype(jnp.bfloat16), "fsdp", scatter_dimension=1, tiled=True
        ).astype(jnp.float32),
        lax.psum_scatter(
            partial_sums[1].astype(jnp.bfloat16), "fsdp", scatter_dimension=1, tiled=True
        ).astype(jnp.float32),
        lax.psum_scatter(
            partial_sums[2].astype(jnp.bfloat16), "fsdp", scatter_dimension=1, tiled=True
        ).astype(jnp.float32),
        lax.psum_scatter(
            partial_sums[3].astype(jnp.bfloat16), "fsdp", scatter_dimension=1, tiled=True
        ).astype(jnp.float32),
        lax.psum_scatter(
            partial_sums[4].astype(jnp.bfloat16), "fsdp", scatter_dimension=1, tiled=True
        ).astype(jnp.float32),
        lax.psum_scatter(
            partial_sums[5].astype(jnp.bfloat16), "fsdp", scatter_dimension=1, tiled=True
        ).astype(jnp.float32),
        lax.psum_scatter(
            partial_sums[6].astype(jnp.bfloat16), "fsdp", scatter_dimension=1, tiled=True
        ).astype(jnp.float32),
        lax.psum_scatter(
            partial_sums[7].astype(jnp.bfloat16), "fsdp", scatter_dimension=1, tiled=True
        ).astype(jnp.float32),
        lax.psum_scatter(
            partial_sums[8].astype(jnp.bfloat16), "fsdp", scatter_dimension=1, tiled=True
        ).astype(jnp.float32),
    )
    mixed = jnp.stack(mixed_parts, axis=0)
    input_grad = jnp.stack(input_parts, axis=0)
    return (
        mixed,
        input_grad,
        reduced[7].reshape(-1),
        reduced[0],
        reduced[1],
        reduced[2],
        reduced[3],
        reduced[8].reshape(-1),
        reduced[4],
        reduced[5],
        reduced[6],
    )


def solution(mesh):
    in_specs = (
        P(None, ("dp", "fsdp"), None),
        P(None, ("dp", "fsdp"), None),
        P(None, "dp", None),
        P("dp"),
        P("dp", "fsdp"),
        P("dp", "fsdp"),
        P("dp", "fsdp"),
        P("dp", "fsdp"),
        P("dp"),
        P("dp", "fsdp"),
        P("dp", "fsdp"),
        P("dp", "fsdp"),
    )
    out_specs = (
        P(None, ("dp", "fsdp"), None),
        P(None, ("dp", "fsdp"), None),
        P("dp"),
        P("dp", "fsdp"),
        P("dp", "fsdp"),
        P("dp", "fsdp"),
        P("dp", "fsdp"),
        P("dp"),
        P("dp", "fsdp"),
        P("dp", "fsdp"),
        P("dp", "fsdp"),
    )
    return jax.shard_map(local, mesh=mesh, in_specs=in_specs, out_specs=out_specs, check_vma=False)
```

profile of v0, /device:TPU:0, one launch (start us, length us, event | category | flops | bytes accessed | tf_op | source)
XLA Modules:
  0.0 1377.6 jit_solution(9324738627138996384)
XLA Ops:
  7.2 8.9 all_gather.58
  34.3 22.5 %all-reduce.9 = (bf16[576]{0:T(1024)(128)(2,1)S(1)}, bf16[576]{0:T(1024)(128)(2,1)}) all-reduce(bf16[576]{0:T(1024)(128)(2,1)S(1)} %dynamic-update-slice, bf16[576]{0:T(1024)(128)(2,1)S(1)} %dynamic-update-slice.1), channel_id=1, replica_groups=mesh['dp'=8,'fsdp'=4] {'dp'}, use_global_device_ids=true, to_apply=%add | all-reduce | flops 1152 | bytes 4608
  69.4 31.3 %all_gather.46 = bf16[576,192]{1,0:T(8,128)(2,1)S(1)} all-gather(bf16[72,192]{1,0:T(8,128)(2,1)S(1)} %copy.192), channel_id=1, replica_groups=mesh['dp'=8,'fsdp'=4] {'dp'}, dimensions={0}, use_global_device_ids=true | all-gather | bytes 248832 | tf_op jit(solution)/shard_map/all_gather | solution.py:233
  104.0 31.4 %all_gather.49 = bf16[576,192]{1,0:T(8,128)(2,1)S(1)} all-gather(bf16[72,192]{1,0:T(8,128)(2,1)S(1)} %copy.193), channel_id=1, replica_groups=mesh['dp'=8,'fsdp'=4] {'dp'}, dimensions={0}, use_global_device_ids=true | all-gather | bytes 248832 | tf_op jit(solution)/shard_map/all_gather | solution.py:232
  145.7 33.2 %all_gather.52 = bf16[576,576]{1,0:T(8,128)(2,1)S(1)} all-gather(bf16[72,576]{1,0:T(8,128)(2,1)S(1)} %copy.196), channel_id=1, replica_groups=mesh['dp'=8,'fsdp'=4] {'dp'}, dimensions={0}, use_global_device_ids=true | all-gather | bytes 746496 | tf_op jit(solution)/shard_map/all_gather | solution.py:231
  205.0 7.7 all_gather.63
  213.5 7.8 all_gather.65
  246.7 32.0 %all_gather.54 = bf16[576,576]{1,0:T(8,128)(2,1)S(1)} all-gather(bf16[72,576]{1,0:T(8,128)(2,1)S(1)} %copy.203), channel_id=1, replica_groups=mesh['dp'=8,'fsdp'=4] {'dp'}, dimensions={0}, use_global_device_ids=true | all-gather | bytes 746496 | tf_op jit(solution)/shard_map/all_gather | solution.py:234
  294.0 12.5 convolution_add_fusion.16
  448.6 17.0 %fusion.18 = (f32[3,3,384]{2,1,0:T(4,128)S(1)}, f32[3,3,384]{2,1,0:T(4,128)S(1)}, f32[3,3,384]{2,1,0:T(4,128)S(1)}, f32[3,3,384]{2,1,0:T(4,128)S(1)}, f32[3,384,384,3]{2,1,3,0:T(8,128)}) fusion(f32[3,384,384,3]{2,1,3,0:T(8,128)} %copy-done.4, f32[3,3,384]{2,1,0:T(4,128)S(1)} %copy-done.179, pred[384,384]{0,1:T(8,128)(4,1)S(1)} %copy-done.81, ...), kind=kOutput, calls=%fused_computation.32 | convolution fusion | flops 196397568 | bytes 43716096 | tf_op jit(solution)/shard_map/tkrd,jkd->krtj/dot_general | solution.py:145
  465.7 15.8 %fusion.23 = (bf16[3,3,384,384]{2,3,1,0:T(8,128)(2,1)S(1)}, bf16[3,3,384,384]{2,3,1,0:T(8,128)(2,1)}, bf16[3,3,384,384]{2,3,1,0:T(8,128)(2,1)S(1)}, bf16[3,3,384,384]{2,3,1,0:T(8,128)(2,1)S(1)}) fusion(f32[3,384,384,3]{2,1,3,0:T(8,128)} %fusion.310, f32[3,384,384,3]{2,1,3,0:T(8,128)} %copy-done.11, f32[3,3,384]{2,1,0:T(4,128)S(1)} %add_add_fusion.6, ...), kind=kLoop, calls=%fused_computation.39 | loop fusion | flops 31850496 | bytes 53701632 | tf_op jit(solution)/shard_map/convert_element_type | solution.py:177
  490.3 15.0 %fusion.6 = (f32[3,3,384]{2,1,0:T(4,128)S(1)}, f32[3,3,384]{2,1,0:T(4,128)S(1)}, f32[3,3,384]{2,1,0:T(4,128)S(1)}, f32[3,3,384]{2,1,0:T(4,128)S(1)}, f32[3,384,384,3]{2,1,3,0:T(8,128)S(1)}) fusion(f32[3,384,384,3]{2,1,3,0:T(8,128)} %copy-done.2, f32[3,3,384]{2,1,0:T(4,128)S(1)} %copy-done.175, pred[384,384]{0,1:T(8,128)(4,1)S(1)} %copy-done.71, ...), kind=kOutput, calls=%fused_computation.12 | convolution fusion | flops 196397568 | bytes 43716096 | tf_op jit(solution)/shard_map/tkrd,jkd->krtj/dot_general | solution.py:145
  505.4 14.5 %fusion.11 = (bf16[3,3,384,384]{2,3,1,0:T(8,128)(2,1)S(1)}, bf16[3,3,384,384]{2,3,1,0:T(8,128)(2,1)S(1)}, bf16[3,3,384,384]{2,3,1,0:T(8,128)(2,1)S(1)}, bf16[3,3,384,384]{2,3,1,0:T(8,128)(2,1)S(1)}) fusion(f32[3,384,384,3]{2,1,3,0:T(8,128)} %fusion.315, f32[3,384,384,3]{2,1,3,0:T(8,128)} %copy-done.8, f32[3,3,384]{2,1,0:T(4,128)S(1)} %add_add_fusion.5, ...), kind=kLoop, calls=%fused_computation.19 | loop fusion | flops 31850496 | bytes 53701632 | tf_op jit(solution)/shard_map/convert_element_type | solution.py:177
  528.0 17.0 %fusion.30 = (f32[3,3,384]{2,1,0:T(4,128)S(1)}, f32[3,3,384]{2,1,0:T(4,128)S(1)}, f32[3,3,384]{2,1,0:T(4,128)S(1)}, f32[3,3,384]{2,1,0:T(4,128)S(1)}, f32[3,384,384,3]{2,1,3,0:T(8,128)}) fusion(f32[3,384,384,3]{2,1,3,0:T(8,128)} %copy-done, f32[3,3,384]{2,1,0:T(4,128)} %log_add_fusion.2, pred[384,384]{0,1:T(8,128)(4,1)S(1)} %copy-done.69, ...), kind=kOutput, calls=%fused_computation.52 | convolution fusion | flops 196397568 | bytes 43716096 | tf_op jit(solution)/shard_map/tkrd,jkd->krtj/dot_general | solution.py:145
  545.1 17.9 %fusion.35 = (bf16[3,3,384,384]{2,3,1,0:T(8,128)(2,1)S(1)}, bf16[3,3,384,384]{2,3,1,0:T(8,128)(2,1)}, bf16[3,3,384,384]{2,3,1,0:T(8,128)(2,1)}, bf16[3,3,384,384]{2,3,1,0:T(8,128)(2,1)}) fusion(f32[3,384,384,3]{2,1,3,0:T(8,128)} %fusion.305, f32[3,384,384,3]{2,1,3,0:T(8,128)} %copy-done.7, f32[3,3,384]{2,1,0:T(4,128)S(1)} %add_add_fusion.7, ...), kind=kLoop, calls=%fused_computation.59 | loop fusion | flops 31850496 | bytes 53701632 | tf_op jit(solution)/shard_map/convert_element_type | solution.py:177
  621.1 23.8 %reduce-scatter.69.cloned.1.call-done = bf16[384,192]{1,0:T(8,128)(2,1)} async-done(((bf16[1536,192]{1,0:T(8,128)(2,1)}), bf16[384,192]{1,0:T(8,128)(2,1)}) %reduce-scatter.69.cloned.1.call-update) | async-done | bytes 147472
  647.3 23.4 %reduce-scatter.73.cloned.1.call-done = bf16[384,192]{1,0:T(8,128)(2,1)} async-done(((bf16[1536,192]{1,0:T(8,128)(2,1)}), bf16[384,192]{1,0:T(8,128)(2,1)}) %reduce-scatter.73.cloned.1.call-update) | async-done | bytes 147472
  673.2 23.5 %reduce-scatter.63.cloned.1.call-done = bf16[384,192]{1,0:T(8,128)(2,1)} async-done(((bf16[1536,192]{1,0:T(8,128)(2,1)}), bf16[384,192]{1,0:T(8,128)(2,1)}) %reduce-scatter.63.cloned.1.call-update) | async-done | bytes 147472
  765.9 60.9 %reduce-scatter.53.cloned.1.call-done = f32[72,192]{1,0:T(8,128)} async-done(((f32[576,192]{1,0:T(8,128)}), f32[72,192]{1,0:T(8,128)}) %reduce-scatter.53.cloned.1.call-update) | async-done | bytes 55312 | tf_op jit(solution)/shard_map/reduce_scatter | solution.py:407
  832.7 59.6 %reduce-scatter.91.cloned.1.call-done = f32[72,576]{1,0:T(8,128)} async-done(((f32[576,576]{1,0:T(8,128)}), f32[72,576]{1,0:T(8,128)}) %reduce-scatter.91.cloned.1.call-update) | async-done | bytes 165904
  894.1 36.0 %all-reduce.8 = (bf16[576,4]{0,1:T(4,128)(2,1)S(1)}, bf16[576,4]{0,1:T(4,128)(2,1)S(1)}) all-reduce(f32[576,4]{0,1:T(4,128)S(1)} %broadcast_in_dim.274, f32[576,4]{0,1:T(4,128)S(1)} %broadcast_in_dim.275), channel_id=8, replica_groups=mesh['dp'=8,'fsdp'=4] {'dp'}, use_global_device_ids=true, to_apply=%region_66.67.clone | all-reduce | flops 4608 | bytes 27648
  930.1 28.2 %reduce-scatter.89.cloned.1.call-done = f32[72,576]{1,0:T(8,128)} async-done(((f32[576,576]{1,0:T(8,128)}), f32[72,576]{1,0:T(8,128)}) %reduce-scatter.89.cloned.1.call-update) | async-done | bytes 165904
  960.1 79.8 %reduce-scatter.57.cloned.1.call-done = f32[72,1536]{1,0:T(8,128)} async-done(((f32[576,1536]{1,0:T(8,128)}), f32[72,1536]{1,0:T(8,128)}) %reduce-scatter.57.cloned.1.call-update) | async-done | bytes 442384 | tf_op jit(solution)/shard_map/reduce_scatter | solution.py:410
  1042.0 80.1 %reduce-scatter.59.cloned.1.call-done = f32[72,1536]{1,0:T(8,128)} async-done(((f32[576,1536]{1,0:T(8,128)}), f32[72,1536]{1,0:T(8,128)}) %reduce-scatter.59.cloned.1.call-update) | async-done | bytes 442384 | tf_op jit(solution)/shard_map/reduce_scatter | solution.py:411
  1128.4 81.2 %reduce-scatter.61.cloned.1.call-done = f32[192,576]{1,0:T(8,128)} async-done(((f32[1536,576]{1,0:T(8,128)}), f32[192,576]{1,0:T(8,128)}) %reduce-scatter.61.cloned.1.call-update) | async-done | bytes 442384 | tf_op jit(solution)/shard_map/reduce_scatter | solution.py:412
  1223.7 8.0 reduce-scatter.79.cloned.1.call-done
  1233.2 20.8 %reduce-scatter.77.cloned.1.call-done = bf16[48,72]{1,0:T(8,128)(2,1)} async-done(((bf16[192,72]{1,0:T(8,128)(2,1)}), bf16[48,72]{1,0:T(8,128)(2,1)}) %reduce-scatter.77.cloned.1.call-update) | async-done | bytes 6928
  1255.5 20.7 %reduce-scatter.81.cloned.1.call-done = bf16[144,72]{1,0:T(8,128)(2,1)} async-done(((bf16[576,72]{1,0:T(8,128)(2,1)}), bf16[144,72]{1,0:T(8,128)(2,1)}) %reduce-scatter.81.cloned.1.call-update) | async-done | bytes 20752
  1277.7 21.2 %reduce-scatter.75.cloned.1.call-done = bf16[144,72]{1,0:T(8,128)(2,1)} async-done(((bf16[576,72]{1,0:T(8,128)(2,1)}), bf16[144,72]{1,0:T(8,128)(2,1)}) %reduce-scatter.75.cloned.1.call-update) | async-done | bytes 20752
  1300.4 22.0 %reduce-scatter.83.cloned.1.call-done = bf16[384,72]{1,0:T(8,128)(2,1)} async-done(((bf16[1536,72]{1,0:T(8,128)(2,1)}), bf16[384,72]{1,0:T(8,128)(2,1)}) %reduce-scatter.83.cloned.1.call-update) | async-done | bytes 55312
  1324.1 21.9 %reduce-scatter.85.cloned.1.call-done = bf16[384,72]{1,0:T(8,128)(2,1)} async-done(((bf16[1536,72]{1,0:T(8,128)(2,1)}), bf16[384,72]{1,0:T(8,128)(2,1)}) %reduce-scatter.85.cloned.1.call-update) | async-done | bytes 55312
  1347.6 21.3 %reduce-scatter.87.cloned.1.call-done = bf16[144,192]{1,0:T(8,128)(2,1)} async-done(((bf16[576,192]{1,0:T(8,128)(2,1)}), bf16[144,192]{1,0:T(8,128)(2,1)}) %reduce-scatter.87.cloned.1.call-update) | async-done | bytes 55312
  (889 shorter events, 440.6 us)
Async XLA Ops:
  7.2 346.5 %all-gather.6.cloned.1.call-start = ((), (), s32[]{:S(2)}) async-start(), calls=%async_computation.21 | async-start | bytes 1990656 | tf_op jit(solution)/shard_map/all_gather | solution.py:236
  16.1 341.7 %all-gather.4.cloned.1.call-start = ((), (), s32[]{:S(2)}) async-start(), calls=%async_computation.20 | async-start | bytes 1990656 | tf_op jit(solution)/shard_map/all_gather | solution.py:235
  22.8 339.0 %all-gather.8.cloned.1.call-start = ((), (), s32[]{:S(2)}) async-start(), calls=%async_computation.22 | async-start | bytes 2211840 | tf_op jit(solution)/shard_map/all_gather | solution.py:237
  30.0 583.5 %reduce-scatter.67.cloned.1.call-start = ((), (), s32[]{:S(2)}) async-start(), calls=%async_computation.30 | async-start | bytes 983040
  56.8 125.7 %copy-start.183 = (f32[576]{0:T(1024)}, f32[576]{0:T(1024)S(1)}, u32[]{:S(2)}) copy-start(f32[576]{0:T(1024)S(1)} %convert_element_type.479) | copy-start | bytes 6916
  246.7 101.1 %copy-start.124 = (bf16[384,192]{0,1:T(8,128)(2,1)}, bf16[384,192]{0,1:T(8,128)(2,1)S(1)}, u32[]{:S(2)}) copy-start(bf16[384,192]{0,1:T(8,128)(2,1)S(1)} %get-tuple-element.151) | copy-start | bytes 442372
  278.7 123.3 %copy-start.39 = (bf16[576,576]{1,0:T(8,128)(2,1)}, bf16[576,576]{1,0:T(8,128)(2,1)S(1)}, u32[]{:S(2)}) copy-start(bf16[576,576]{1,0:T(8,128)(2,1)S(1)} %all_gather.54) | copy-start | bytes 1990660
  280.3 114.4 %copy-start.65 = (pred[384,384]{0,1:T(8,128)(4,1)}, pred[384,384]{0,1:T(8,128)(4,1)S(1)}, u32[]{:S(2)}) copy-start(pred[384,384]{0,1:T(8,128)(4,1)S(1)} %get-tuple-element.229) | copy-start | bytes 442372
  490.2 125.0 %reduce-scatter.71.cloned.1.call-start = ((), (), s32[]{:S(2)}) async-start(), calls=%async_computation.32 | async-start | bytes 983040
  572.6 46.4 %reduce-scatter.65.cloned.1.call-start = ((), (), s32[]{:S(2)}) async-start(), calls=%async_computation.29 | async-start | bytes 983040
  580.1 64.8 %reduce-scatter.69.cloned.1.call-start = ((), (), s32[]{:S(2)}) async-start(), calls=%async_computation.31 | async-start | bytes 983040
  596.8 73.9 %reduce-scatter.73.cloned.1.call-start = ((), (), s32[]{:S(2)}) async-start(), calls=%async_computation.33 | async-start | bytes 983040
  604.9 91.8 %reduce-scatter.63.cloned.1.call-start = ((), (), s32[]{:S(2)}) async-start(), calls=%async_computation.28 | async-start | bytes 983040
  613.2 148.8 %reduce-scatter.55.cloned.1.call-start = ((), (), s32[]{:S(2)}) async-start(), calls=%async_computation.24 | async-start | bytes 663552 | tf_op jit(solution)/shard_map/reduce_scatter | solution.py:408
  673.1 153.6 %reduce-scatter.53.cloned.1.call-start = ((), (), s32[]{:S(2)}) async-start(), calls=%async_computation.23 | async-start | bytes 663552 | tf_op jit(solution)/shard_map/reduce_scatter | solution.py:407
  702.2 190.1 %reduce-scatter.91.cloned.1.call-start = ((), (), s32[]{:S(2)}) async-start(), calls=%async_computation.42 | async-start | bytes 1658880
  708.8 249.5 %reduce-scatter.89.cloned.1.call-start = ((), (), s32[]{:S(2)}) async-start(), calls=%async_computation.41 | async-start | bytes 1658880
  719.5 320.5 %reduce-scatter.57.cloned.1.call-start = ((), (), s32[]{:S(2)}) async-start(), calls=%async_computation.25 | async-start | bytes 3981312 | tf_op jit(solution)/shard_map/reduce_scatter | solution.py:410
  726.1 396.0 %reduce-scatter.59.cloned.1.call-start = ((), (), s32[]{:S(2)}) async-start(), calls=%async_computation.26 | async-start | bytes 3981312 | tf_op jit(solution)/shard_map/reduce_scatter | solution.py:411
  732.8 476.8 %reduce-scatter.61.cloned.1.call-start = ((), (), s32[]{:S(2)}) async-start(), calls=%async_computation.27 | async-start | bytes 4423680 | tf_op jit(solution)/shard_map/reduce_scatter | solution.py:412
  741.8 489.9 %reduce-scatter.79.cloned.1.call-start = ((), (), s32[]{:S(2)}) async-start(), calls=%async_computation.36 | async-start | bytes 61440
  758.4 135.6 %copy-start.205 = (f32[576]{0:T(1024)S(1)}, f32[576]{0:T(1024)}, u32[]{:S(2)}) copy-start(f32[576]{0:T(1024)} %add_add_fusion.8) | copy-start | bytes 6916
  763.6 490.3 %reduce-scatter.77.cloned.1.call-start = ((), (), s32[]{:S(2)}) async-start(), calls=%async_computation.35 | async-start | bytes 61440
  828.4 295.9 %copy-start.37 = (f32[384,576]{0,1:T(8,128)S(1)}, f32[384,576]{0,1:T(8,128)}, u32[]{:S(2)}) copy-start(f32[384,576]{0,1:T(8,128)} %copy-done.36) | copy-start | bytes 2654212
  828.4 295.9 %copy-start.206 = (f32[384]{0:T(512)S(1)}, f32[384]{0:T(512)}, u32[]{:S(2)}) copy-start(f32[384]{0:T(512)} %get-tuple-element.246) | copy-start | bytes 4612
  828.4 295.9 %copy-start.217 = (f32[384]{0:T(512)S(1)}, f32[384]{0:T(512)}, u32[]{:S(2)}) copy-start(f32[384]{0:T(512)} %get-tuple-element.250) | copy-start | bytes 4612
  828.4 295.9 %copy-start.218 = (f32[384]{0:T(512)S(1)}, f32[384]{0:T(512)}, u32[]{:S(2)}) copy-start(f32[384]{0:T(512)} %get-tuple-element.315) | copy-start | bytes 4612
  828.4 447.8 %reduce-scatter.81.cloned.1.call-start = ((), (), s32[]{:S(2)}) async-start(), calls=%async_computation.37 | async-start | bytes 184320
  894.0 404.9 %reduce-scatter.75.cloned.1.call-start = ((), (), s32[]{:S(2)}) async-start(), calls=%async_computation.34 | async-start | bytes 184320
  960.1 362.3 %reduce-scatter.83.cloned.1.call-start = ((), (), s32[]{:S(2)}) async-start(), calls=%async_computation.38 | async-start | bytes 491520
  1041.9 304.0 %reduce-scatter.85.cloned.1.call-start = ((), (), s32[]{:S(2)}) async-start(), calls=%async_computation.39 | async-start | bytes 491520
  1124.1 244.8 %reduce-scatter.87.cloned.1.call-start = ((), (), s32[]{:S(2)}) async-start(), calls=%async_computation.40 | async-start | bytes 368640
  (252 other events, 4310.5 us)
Sparse Core Ops, SparseCore 0:
  16.3 46.4 all-gather.5
  65.0 47.6 all-gather.3
  114.9 54.4 all-gather.7
  490.3 20.4 reduce-scatter.66
  572.7 20.5 reduce-scatter.70
  595.7 23.2 reduce-scatter.64
  621.7 23.2 reduce-scatter.68
  647.5 23.2 reduce-scatter.72
  673.4 23.2 reduce-scatter.62
  699.9 62.1 reduce-scatter.54
  765.7 61.0 reduce-scatter.52
  830.1 62.0 reduce-scatter.90
  896.3 61.9 reduce-scatter.88
  961.8 78.0 reduce-scatter.56
  1043.4 78.6 reduce-scatter.58
  1125.7 83.8 reduce-scatter.60
  1212.6 19.0 reduce-scatter.78
  1234.6 19.3 reduce-scatter.76
  1256.5 19.6 reduce-scatter.80
  1279.2 19.6 reduce-scatter.74
  1301.5 20.8 reduce-scatter.82
  1325.1 20.8 reduce-scatter.84
  1348.6 20.2 reduce-scatter.86
where the time goes:
time: 1390 us; the launch traced here: 1380 us
  waiting for transfers between devices  601 us (43%)
  matrix products  315 us (23%)
  blocking collectives  282 us (20%)
  other arithmetic  113 us (8%)
  local copies, waits for them, and re-layouts  46.1 us (3%)
  between operations  19.9 us (1%)
    unnamed x38, waiting for transfers between devices  295 us
    dot_general x12, matrix products, attend_backward(): jnp.einsum('tkrd,jkd->krtj', grad_attended, values_all[first_row:last_row...  82.3 us
    reduce_scatter x1, waiting for transfers between devices, local(): lax.psum_scatter(grad_down, 'dp', scatter_dimension=0, tiled=True)  81.2 us
    reduce_scatter x1, waiting for transfers between devices, local(): lax.psum_scatter(grad_up, 'dp', scatter_dimension=0, tiled=True)  80.1 us
    reduce_scatter x1, waiting for transfers between devices, local(): lax.psum_scatter(grad_gate, 'dp', scatter_dimension=0, tiled=True)  79.8 us
    unnamed x3, blocking collectives  64.8 us
    reduce_scatter x1, waiting for transfers between devices, local(): lax.psum_scatter(grad_key, 'dp', scatter_dimension=0, tiled=True)  60.9 us
    convert_element_type x3, other arithmetic, attend_backward(): dscores = (probs * (dprobs - row_dots[..., None])).astype(jnp.bfloat16)  48.2 us
  transfers between devices with their start and end apart: 23, of which 18 were waited for; matrix products, arithmetic and copies ran while one was open for 25% of the time, Pallas kernels for 0%

commit v1 on v0

v1 whole, which is shorter than its diff:
```python
import functools
import math

import jax
import jax.numpy as jnp
from jax import lax
from jax.experimental import pallas as pl
from jax.experimental.pallas import tpu as pltpu
from jax.sharding import PartitionSpec as P

HEADS = 9
KV_HEADS = 3
HEAD_DIM = 64
FF = 1536
REPEATS = HEADS // KV_HEADS
QW = HEADS * HEAD_DIM
KW = KV_HEADS * HEAD_DIM
EPSILON = 1e-05
ROPE_BASE = 100000.0
MASKED = -1e30
BOTH = ("dp", "fsdp")
F32 = jnp.float32
BF16 = jnp.bfloat16


def dot(a, b):
    return lax.dot_general(a, b, (((1,), (0,)), ((), ())), preferred_element_type=F32)


def dot_nt(a, b):
    return lax.dot_general(a, b, (((1,), (1,)), ((), ())), preferred_element_type=F32)


def dot_tn(a, b):
    return lax.dot_general(a, b, (((0,), (0,)), ((), ())), preferred_element_type=F32)


def params(mib=56):
    return pltpu.CompilerParams(vmem_limit_bytes=mib << 20)


def whole(count):
    return [pl.BlockSpec(memory_space=pltpu.VMEM)] * count


def pack_attention(w_query, w_key, w_value, w_out, gain_one, gain_two):
    rows = w_query.shape[0]
    body = jnp.concatenate([w.astype(F32) for w in (w_query, w_key, w_value, w_out)], axis=1)
    lanes = body.shape[1]
    extra = padded_rows(rows) - rows
    gains = jnp.concatenate(
        [
            gain_one.astype(F32),
            gain_two.astype(F32),
            jnp.zeros((1, lanes - 2 * rows), F32),
        ],
        axis=1,
    )
    gains = jnp.broadcast_to(gains, (extra, lanes))
    return jnp.concatenate([body, gains], axis=0).astype(BF16)


def padded_rows(rows):
    return -(-(rows + 1) // 16) * 16


def pack_down(w_down, rows):
    turned = w_down.astype(F32).T
    pieces = turned.shape[0] // rows
    return jnp.concatenate(
        [turned[n * rows : (n + 1) * rows] for n in range(pieces)], axis=1
    ).astype(BF16)


def unpack_attention(block, rows, q_cols, k_cols):
    block = block.astype(F32)
    ends = (0, q_cols, q_cols + k_cols, q_cols + 2 * k_cols, 2 * q_cols + 2 * k_cols)
    parts = [block[:rows, ends[n] : ends[n + 1]] for n in range(4)]
    return parts + [block[rows : rows + 1, :rows], block[rows : rows + 1, rows : 2 * rows]]


def unpack_down(block, shape):
    block = block.astype(F32)
    lanes = shape[0]
    pieces = block.shape[1] // lanes
    return jnp.concatenate(
        [block[:, n * lanes : (n + 1) * lanes] for n in range(pieces)], axis=0
    ).T


def pack_kernel(q, k, v, o, one, two, gate, up, down, attn_ref, ffn_ref):
    attn_ref[...] = pack_attention(q[...], k[...], v[...], o[...], one[...], two[...])
    ffn_ref[0] = gate[...]
    ffn_ref[1] = up[...]
    ffn_ref[2] = pack_down(down[...], gate.shape[0])


def unpack_kernel(attn, ffn, q, k, v, o, one, two, gate, up, down):
    rows = gate.shape[0]
    parts = unpack_attention(attn[...], rows, q.shape[1], k.shape[1])
    for ref, part in zip((q, k, v, o, one, two), parts, strict=True):
        ref[...] = part
    gate[...] = ffn[0].astype(F32)
    up[...] = ffn[1].astype(F32)
    down[...] = unpack_down(ffn[2], down.shape)


def attention_rows(block_of, number, members, rows, q_cols, k_cols):
    blocks = [block_of(number * members + f).astype(F32) for f in range(members)]
    ends = (0, q_cols, q_cols + k_cols, q_cols + 2 * k_cols, 2 * q_cols + 2 * k_cols)
    spans = [
        jnp.concatenate([b[:rows, ends[n] : ends[n + 1]] for b in blocks], axis=1)
        for n in range(4)
    ]
    gains = (blocks[0][rows : rows + 1, :rows], blocks[0][rows : rows + 1, rows : 2 * rows])
    return jnp.concatenate(spans[:3], axis=1), spans[3], gains


def join_attention_kernel(members, rows, q_cols, k_cols, g_ref, wqkv_ref, wo_ref, one_ref, two_ref):
    parts = g_ref.shape[0] // members
    gains = []
    for pair in range(parts // 2):
        made = [
            attention_rows(lambda n: g_ref[n], 2 * pair + s, members, rows, q_cols, k_cols)
            for s in range(2)
        ]
        gains += [m[2] for m in made]
        span = slice(pair * 2 * rows, (pair + 1) * 2 * rows)
        wqkv_ref[span, :] = jnp.concatenate([m[0] for m in made], axis=0).astype(BF16)
        wo_ref[span, :] = jnp.concatenate([m[1] for m in made], axis=0).astype(BF16)
    one_ref[...] = jnp.concatenate([g[0] for g in gains], axis=1)
    two_ref[...] = jnp.concatenate([g[1] for g in gains], axis=1)


def join_attention_plain(members, rows, q_cols, k_cols, gathered):
    parts = gathered.shape[0] // members
    made = [
        attention_rows(lambda n: gathered[n], s, members, rows, q_cols, k_cols)
        for s in range(parts)
    ]
    return (
        jnp.concatenate([m[0] for m in made], axis=0).astype(BF16),
        jnp.concatenate([m[1] for m in made], axis=0).astype(BF16),
        jnp.concatenate([m[2][0] for m in made], axis=1),
        jnp.concatenate([m[2][1] for m in made], axis=1),
    )


def join_ffn_kernel(members, g_ref, gate_ref, up_ref, down_ref):
    rows, lanes = g_ref.shape[2:]
    pairs = g_ref.shape[0] // members // 2
    half = lanes // 2
    for pair in range(pairs):
        for f in range(members):
            first = 2 * pair * members + f
            second = first + members
            for which, ref in ((0, gate_ref), (1, up_ref)):
                both = [g_ref[n, which].astype(F32) for n in (first, second)]
                ref[
                    pair * 2 * rows : (pair + 1) * 2 * rows, f * lanes : (f + 1) * lanes
                ] = jnp.concatenate(both, axis=0).astype(BF16)
            a, b = (g_ref[n, 2].astype(F32) for n in (first, second))
            top = jnp.concatenate([a[:, :half], b[:, :half]], axis=1)
            low = jnp.concatenate([a[:, half:], b[:, half:]], axis=1)
            down_ref[f * 2 * rows : (f + 1) * 2 * rows, pair * lanes : (pair + 1) * lanes] = (
                jnp.concatenate([top, low], axis=0).astype(BF16)
            )


def join_ffn_plain(members, gathered):
    rows, lanes = gathered.shape[2:]
    parts = gathered.shape[0] // members
    width = rows * parts
    g = gathered.reshape(parts, members, 3, rows, lanes)
    across = [
        g[:, :, n].transpose(0, 2, 1, 3).reshape(width, members * lanes) for n in range(2)
    ]
    deep = FF // parts
    down = g[:, :, 2].reshape(parts, members, rows, lanes // deep, deep)
    down = down.transpose(1, 3, 2, 0, 4).reshape(width, FF)
    return across[0], across[1], down


def swap_halves(chunk):
    lane = lax.broadcasted_iota(jnp.int32, chunk.shape, 1)
    low = (lane % HEAD_DIM) < HEAD_DIM // 2
    return jnp.where(low, pltpu.roll(chunk, 96, 1), pltpu.roll(chunk, 32, 1))


def turn(vectors, cosine, sine):
    chunks = []
    for n in range(vectors.shape[1] // 128):
        chunk = vectors[:, n * 128 : (n + 1) * 128]
        chunks.append(chunk * cosine + swap_halves(chunk) * sine)
    return jnp.concatenate(chunks, axis=1)


def norm_scale(values):
    return lax.rsqrt(jnp.mean(values * values, axis=1, keepdims=True) + EPSILON)


def norm_back(inputs, scale, gain, grads):
    weighted = grads * gain
    term = jnp.sum(grads * (inputs * scale), axis=0, keepdims=True)
    cubed = scale * scale * scale
    mean = jnp.mean(weighted * inputs, axis=1, keepdims=True)
    return scale * weighted - inputs * (cubed * mean), term


def pre_kernel(x_ref, w_ref, gain_ref, cos_ref, sin_ref, q_ref, kv_ref):
    x = x_ref[...].astype(F32)
    normed = (x * norm_scale(x) * gain_ref[...]).astype(BF16)
    raw = dot(normed, w_ref[...])
    turned = turn(raw[:, : QW + KW], cos_ref[...], sin_ref[...])
    q_ref[...] = (turned[:, :QW].astype(BF16).astype(F32) * HEAD_DIM**-0.5).astype(BF16)
    kv_ref[...] = jnp.concatenate([turned[:, QW:], raw[:, QW + KW :]], axis=1).astype(BF16)


def row_range(lens_ref, micro, first_row, rows):
    end_zero = lens_ref[micro, 0]
    end_one = end_zero + lens_ref[micro, 1]
    end_two = end_one + lens_ref[micro, 2]
    places = first_row + lax.broadcasted_iota(jnp.int32, (1, rows), 1)

    def begin(at):
        return jnp.where(
            at < end_zero, 0, jnp.where(at < end_one, end_zero, jnp.where(at < end_two, end_one, at))
        )

    return places, begin(places), begin(first_row)


def mask_of(key_block, rows, places, begins):
    keys = key_block * rows + lax.broadcasted_iota(jnp.int32, (rows, rows), 0)
    bias = jnp.where((keys >= begins) & (keys <= places), 0.0, MASKED)
    return jnp.concatenate([bias] * REPEATS, axis=1)


def stacked(values, group):
    first = group * REPEATS
    return jnp.concatenate(
        [
            values[:, (first + n) * HEAD_DIM : (first + n + 1) * HEAD_DIM]
            for n in range(REPEATS)
        ],
        axis=0,
    )


def unstacked(groups):
    rows = groups[0].shape[0] // REPEATS
    return jnp.concatenate(
        [g[n * rows : (n + 1) * rows] for g in groups for n in range(REPEATS)], axis=1
    )


def head_of(values, number):
    return values[:, number * HEAD_DIM : (number + 1) * HEAD_DIM]


def forward_kernel(lens_ref, place_ref, q_ref, kv_ref, out_ref, lse_ref, acc, top, total):
    micro = pl.program_id(0)
    rows = q_ref.shape[1]
    member = place_ref[0]
    places, begins, lowest = row_range(lens_ref, micro, member * rows, rows)
    queries = [stacked(q_ref[0], g) for g in range(KV_HEADS)]
    acc[...] = jnp.zeros_like(acc)
    top[...] = jnp.full_like(top, MASKED)
    total[...] = jnp.zeros_like(total)

    def block(number, carry):
        bias = mask_of(number, rows, places, begins)
        kv = kv_ref[number, 0]
        for g in range(KV_HEADS):
            keys, values = head_of(kv, g), head_of(kv, KV_HEADS + g)
            scores = dot_nt(keys, queries[g]) + bias
            before = top[g]
            now = jnp.maximum(before, jnp.max(scores, axis=0, keepdims=True))
            shrink = jnp.exp(before - now)
            weights = jnp.exp(scores - now)
            total[g] = total[g] * shrink + jnp.sum(weights, axis=0, keepdims=True)
            acc[g] = acc[g] * shrink + dot_tn(values, weights.astype(BF16))
            top[g] = now
        return carry

    lax.fori_loop(lowest // rows, member + 1, block, 0)
    done = []
    for g in range(KV_HEADS):
        done.append((acc[g] * (1.0 / total[g])).T)
        lse_ref[0, g] = top[g] + jnp.log(total[g])
    out_ref[0] = unstacked(done)


def backward_kernel(
    lens_ref, place_ref, q_ref, kv_ref, out_ref, grad_ref, lse_ref, dq_ref, dkv_ref, acc
):
    micro = pl.program_id(0)
    rows = q_ref.shape[1]
    member = place_ref[0]
    places, begins, lowest = row_range(lens_ref, micro, member * rows, rows)
    queries = [stacked(q_ref[0], g) for g in range(KV_HEADS)]
    grads = [stacked(grad_ref[0], g) for g in range(KV_HEADS)]
    product = grad_ref[0].astype(F32) * out_ref[0]
    dots = [
        jnp.sum(stacked(product, g).T, axis=0, keepdims=True) for g in range(KV_HEADS)
    ]
    acc[...] = jnp.zeros_like(acc)
    dkv_ref[...] = jnp.zeros_like(dkv_ref)

    def block(number, carry):
        bias = mask_of(number, rows, places, begins)
        kv = kv_ref[number, 0]
        grad_keys, grad_values = [], []
        for g in range(KV_HEADS):
            keys, values = head_of(kv, g), head_of(kv, KV_HEADS + g)
            probs = jnp.exp(dot_nt(keys, queries[g]) + bias - lse_ref[0, g])
            grad_probs = dot_nt(values, grads[g])
            grad_scores = (probs * (grad_probs - dots[g])).astype(BF16)
            grad_values.append(dot(probs.astype(BF16), grads[g]))
            grad_keys.append(dot(grad_scores, queries[g]))
            acc[g] = acc[g] + dot_tn(keys, grad_scores)
        dkv_ref[number, 0] = jnp.concatenate(grad_keys + grad_values, axis=1).astype(BF16)
        return carry

    lax.fori_loop(lowest // rows, member + 1, block, 0)
    dq_ref[0] = unstacked([acc[g].T for g in range(KV_HEADS)]) * HEAD_DIM**-0.5


def mid_kernel(
    members,
    as_blocks,
    x_ref,
    att_ref,
    dy_ref,
    wo_ref,
    gate_ref,
    up_ref,
    down_ref,
    gain_ref,
    mixed_ref,
    dmid_ref,
    datt_ref,
    gout_ref,
    gffn_ref,
    ggain_ref,
    s_hidden,
    s_dgate,
    s_dup,
    s_branch,
    s_normed,
    s_dy,
    s_att,
):
    step = pl.program_id(0)
    rows = x_ref.shape[0]
    here = pl.ds(pl.multiple_of(step * rows, rows), rows)
    gain = gain_ref[...]
    att = att_ref[...].astype(BF16)
    middle = x_ref[...].astype(F32) + dot(att, wo_ref[...])
    scale = norm_scale(middle)
    normed = (middle * scale * gain).astype(BF16)
    gate = dot(normed, gate_ref[...])
    up = dot(normed, up_ref[...])
    sig = lax.logistic(gate)
    silu = gate * sig
    hidden = (silu * up).astype(BF16)
    mixed_ref[...] = (middle + dot_nt(hidden, down_ref[...])).astype(BF16)
    dy = dy_ref[...]
    dhidden = dot(dy, down_ref[...])
    dgate = (dhidden * up * sig * (1.0 + gate * (1.0 - sig))).astype(BF16)
    dup = (dhidden * silu).astype(BF16)
    dnormed = dot_nt(dgate, gate_ref[...]) + dot_nt(dup, up_ref[...])
    back, term = norm_back(middle, scale, gain, dnormed)
    dmid = dy.astype(F32) + back
    dmid_ref[...] = dmid
    branch = dmid.astype(BF16)
    datt_ref[...] = dot_nt(branch, wo_ref[...]).astype(BF16)
    s_hidden[here, :] = hidden
    s_dgate[here, :] = dgate
    s_dup[here, :] = dup
    s_branch[here, :] = branch
    s_normed[here, :] = normed
    s_dy[here, :] = dy
    s_att[here, :] = att

    @pl.when(step == 0)
    def _():
        ggain_ref[...] = term

    @pl.when(step > 0)
    def _():
        ggain_ref[...] += term

    @pl.when(step == pl.num_programs(0) - 1)
    def _():
        width = s_normed.shape[1]
        gout_ref[...] = dot_tn(s_att[...], s_branch[...])
        normed_t = s_normed[...].T
        dy_t = s_dy[...].T
        if not as_blocks:
            gffn_ref[0] = dot(normed_t, s_dgate[...]).astype(BF16)
            gffn_ref[1] = dot(normed_t, s_dup[...]).astype(BF16)
            gffn_ref[2] = dot(dy_t, s_hidden[...]).astype(BF16)
            return
        parts = gffn_ref.shape[0] // members
        part = width // parts
        lanes = FF // members
        deep = FF // parts
        for f in range(members):
            for which, src in ((0, s_dgate), (1, s_dup)):
                made = dot(normed_t, src[:, f * lanes : (f + 1) * lanes])
                for n in range(parts):
                    gffn_ref[n * members + f, which] = made[n * part : (n + 1) * part].astype(BF16)
            cols = width // members
            made = dot(dy_t[f * cols : (f + 1) * cols], s_hidden[...])
            for n in range(parts):
                span = made[:, n * deep : (n + 1) * deep]
                gffn_ref[n * members + f, 2] = jnp.concatenate(
                    [span[i * part : (i + 1) * part] for i in range(cols // part)], axis=1
                ).astype(BF16)


def blocks_of_ffn(full, members, parts):
    width = full.shape[1]
    part, lanes, deep = width // parts, FF // members, FF // parts
    across = full[:2].reshape(2, parts, part, members, lanes).transpose(1, 3, 0, 2, 4)
    cols = width // members
    down = full[2].reshape(members, cols // part, part, parts, deep).transpose(3, 0, 2, 1, 4)
    across = across.reshape(parts * members, 2, part, lanes)
    down = down.reshape(parts * members, 1, part, lanes)
    return jnp.concatenate([across, down], axis=1)


def attention_blocks(grad_qkv, grad_out, gain_one, gain_two, members, parts, store):
    width = grad_qkv.shape[0]
    part = width // parts
    q_cols, k_cols = QW // members, KW // members
    extra = padded_rows(part) - part
    lanes = 2 * q_cols + 2 * k_cols
    for n in range(parts):
        rows = slice(n * part, (n + 1) * part)
        gains = jnp.concatenate(
            [gain_one[:, rows], gain_two[:, rows], jnp.zeros((1, lanes - 2 * part), F32)], axis=1
        )
        gains = jnp.broadcast_to(gains, (extra, lanes))
        for f in range(members):
            spans = [
                grad_qkv[rows, f * q_cols : (f + 1) * q_cols],
                grad_qkv[rows, QW + f * k_cols : QW + (f + 1) * k_cols],
                grad_qkv[rows, QW + KW + f * k_cols : QW + KW + (f + 1) * k_cols],
                grad_out[rows, f * q_cols : (f + 1) * q_cols],
            ]
            body = jnp.concatenate(spans, axis=1)
            store(n * members + f, jnp.concatenate([body, gains], axis=0).astype(BF16))


def post_kernel(
    members,
    as_blocks,
    x_ref,
    dq_ref,
    dkv_ref,
    dmid_ref,
    w_ref,
    gain_ref,
    cos_ref,
    sin_ref,
    gout_ref,
    ggain_ref,
    dx_ref,
    gattn_ref,
    gone_ref,
    s_raw,
    s_normed,
):
    step = pl.program_id(0)
    rows = x_ref.shape[0]
    here = pl.ds(pl.multiple_of(step * rows, rows), rows)
    gain = gain_ref[...]
    x = x_ref[...].astype(F32)
    scale = norm_scale(x)
    s_normed[here, :] = (x * scale * gain).astype(BF16)
    dkv = dkv_ref[...].astype(F32)
    turned = jnp.concatenate([dq_ref[...], dkv[:, :KW]], axis=1)
    turned = turn(turned, cos_ref[...], -sin_ref[...])
    raw = jnp.concatenate([turned, dkv[:, KW:]], axis=1).astype(BF16)
    s_raw[here, :] = raw
    back, term = norm_back(x, scale, gain, dot_nt(raw, w_ref[...]))
    dx_ref[...] = dmid_ref[...] + back

    @pl.when(step == 0)
    def _():
        gone_ref[...] = term

    @pl.when(step > 0)
    def _():
        gone_ref[...] += term

    @pl.when(step == pl.num_programs(0) - 1)
    def _():
        grad_qkv = dot_tn(s_normed[...], s_raw[...])
        if not as_blocks:
            gattn_ref[...] = grad_qkv
            return

        def store(number, block):
            gattn_ref[number] = block

        parts = gattn_ref.shape[0] // members
        attention_blocks(
            grad_qkv, gout_ref[...], gone_ref[...], ggain_ref[...], members, parts, store
        )


def shape_of(shape, dtype):
    return jax.ShapeDtypeStruct(shape, dtype)


def gather_blocks(block):
    return lax.all_gather(block, BOTH, axis=0, tiled=False)


def scatter_blocks(blocks):
    return lax.psum_scatter(blocks, BOTH, scatter_dimension=0, tiled=False)


def local(
    tokens,
    cotangent,
    lengths,
    gain_attn,
    w_query,
    w_key,
    w_value,
    w_out,
    gain_mlp,
    w_gate,
    w_up,
    w_down,
):
    members = lax.axis_size("fsdp")
    parts = lax.axis_size("dp")
    count = parts * members
    member = lax.axis_index("fsdp")
    micro, rows, width = tokens.shape
    every = micro * rows
    part = w_query.shape[0]
    q_cols, k_cols = w_query.shape[1], w_key.shape[1]
    lanes = w_gate.shape[1]
    deep = padded_rows(part)
    as_blocks = part % 8 == 0 and parts % 2 == 0 and width // members == 2 * part

    lens = lengths[:, 0, :]
    place = jnp.reshape(member, (1,)).astype(jnp.int32)
    ends = jnp.cumsum(lens, axis=1)
    at = member * rows + lax.broadcasted_iota(jnp.int32, (micro, rows), 1)
    begins = jnp.zeros_like(at)
    for n in range(lens.shape[1]):
        following = ends[:, n : n + 1] if n < lens.shape[1] - 1 else at
        begins = jnp.where(ends[:, n : n + 1] <= at, following, begins)
    posit = (at - begins).reshape(every, 1).astype(F32)
    lane = lax.broadcasted_iota(jnp.int32, (1, 128), 1)
    halfway = HEAD_DIM // 2
    freqs = jnp.exp((lane % halfway).astype(F32) * (-math.log(ROPE_BASE) / halfway))
    angles = posit * freqs
    cosine = jnp.cos(angles)
    sine = jnp.sin(angles) * jnp.where(lane % HEAD_DIM < halfway, -1.0, 1.0)

    gain_rows = (gain_attn.reshape(1, part), gain_mlp.reshape(1, part))
    own = (w_query, w_key, w_value, w_out) + gain_rows
    if as_blocks:
        attn_block, ffn_block = pl.pallas_call(
            pack_kernel,
            out_shape=(shape_of((deep, lanes), BF16), shape_of((3, part, lanes), BF16)),
            in_specs=whole(9),
            out_specs=whole(2),
            compiler_params=params(),
            name="pack",
        )(*own, w_gate, w_up, w_down)
    else:
        attn_block = pack_attention(*own)
        ffn_block = jnp.stack([w_gate, w_up, pack_down(w_down, part)])
    attn_all = gather_blocks(attn_block)
    ffn_all = gather_blocks(ffn_block)
    if as_blocks:
        wqkv, wo, gain_one, gain_two = pl.pallas_call(
            functools.partial(join_attention_kernel, members, part, q_cols, k_cols),
            out_shape=(
                shape_of((width, QW + 2 * KW), BF16),
                shape_of((QW, width), BF16),
                shape_of((1, width), F32),
                shape_of((1, width), F32),
            ),
            in_specs=whole(1),
            out_specs=whole(4),
            compiler_params=params(),
            name="join_attention",
        )(attn_all)
        gate_w, up_w, down_w = pl.pallas_call(
            functools.partial(join_ffn_kernel, members),
            out_shape=(shape_of((width, FF), BF16),) * 3,
            in_specs=whole(1),
            out_specs=whole(3),
            compiler_params=params(),
            name="join_ffn",
        )(ffn_all)
    else:
        wqkv, wo, gain_one, gain_two = join_attention_plain(
            members, part, q_cols, k_cols, attn_all
        )
        gate_w, up_w, down_w = join_ffn_plain(members, ffn_all)

    x = tokens.reshape(every, width)
    dy = cotangent.reshape(every, width)

    def by_rows(cols):
        return pl.BlockSpec((rows, cols), lambda n: (n, 0))

    def same(*shape):
        return pl.BlockSpec(shape, lambda n: (0,) * len(shape))

    queries, own_kv = pl.pallas_call(
        pre_kernel,
        grid=(micro,),
        out_shape=(shape_of((every, QW), BF16), shape_of((every, 2 * KW), BF16)),
        in_specs=[
            by_rows(width),
            same(width, QW + 2 * KW),
            same(1, width),
            by_rows(128),
            by_rows(128),
        ],
        out_specs=(by_rows(QW), by_rows(2 * KW)),
        compiler_params=params(),
        name="pre",
    )(x, wqkv, gain_one, cosine, sine)

    kv_all = lax.all_gather(own_kv, "fsdp", axis=0, tiled=False)
    kv_all = kv_all.reshape(members, micro, rows, 2 * KW)
    queries = queries.reshape(micro, rows, QW)

    smem = pl.BlockSpec(memory_space=pltpu.SMEM)
    by_micro = pl.BlockSpec((1, rows, QW), lambda n: (n, 0, 0))
    by_kv = pl.BlockSpec((members, 1, rows, 2 * KW), lambda n: (0, n, 0, 0))
    by_lse = pl.BlockSpec((1, KV_HEADS, 1, REPEATS * rows), lambda n: (n, 0, 0, 0))
    held = (KV_HEADS, HEAD_DIM, REPEATS * rows)
    line = (KV_HEADS, 1, REPEATS * rows)
    attended, logsum = pl.pallas_call(
        forward_kernel,
        grid=(micro,),
        out_shape=(shape_of((micro, rows, QW), F32), shape_of((micro,) + line, F32)),
        in_specs=[smem, smem, by_micro, by_kv],
        out_specs=(by_micro, by_lse),
        scratch_shapes=[pltpu.VMEM(held, F32), pltpu.VMEM(line, F32), pltpu.VMEM(line, F32)],
        compiler_params=params(),
        name="attend_forward",
    )(lens, place, queries, kv_all)

    if as_blocks:
        gffn_shape = (count, 3, part, lanes)
    else:
        gffn_shape = (3, width, FF)
    mixed, dmid, datt, grad_out, grad_ffn, grad_two = pl.pallas_call(
        functools.partial(mid_kernel, members, as_blocks),
        grid=(micro,),
        out_shape=(
            shape_of((every, width), BF16),
            shape_of((every, width), F32),
            shape_of((every, QW), BF16),
            shape_of((QW, width), F32),
            shape_of(gffn_shape, BF16),
            shape_of((1, width), F32),
        ),
        in_specs=[
            by_rows(width),
            by_rows(QW),
            by_rows(width),
            same(QW, width),
            same(width, FF),
            same(width, FF),
            same(width, FF),
            same(1, width),
        ],
        out_specs=(
            by_rows(width),
            by_rows(width),
            by_rows(QW),
            same(QW, width),
            same(*gffn_shape),
            same(1, width),
        ),
        scratch_shapes=[
            pltpu.VMEM((every, FF), BF16),
            pltpu.VMEM((every, FF), BF16),
            pltpu.VMEM((every, FF), BF16),
            pltpu.VMEM((every, width), BF16),
            pltpu.VMEM((every, width), BF16),
            pltpu.VMEM((every, width), BF16),
            pltpu.VMEM((every, QW), BF16),
        ],
        compiler_params=params(),
        name="mid",
    )(x, attended.reshape(every, QW), dy, wo, gate_w, up_w, down_w, gain_two)

    if not as_blocks:
        grad_ffn = blocks_of_ffn(grad_ffn, members, parts)
    ffn_sum = scatter_blocks(grad_ffn)

    dq, dkv = pl.pallas_call(
        backward_kernel,
        grid=(micro,),
        out_shape=(
            shape_of((micro, rows, QW), F32),
            shape_of((members, micro, rows, 2 * KW), BF16),
        ),
        in_specs=[smem, smem, by_micro, by_kv, by_micro, by_micro, by_lse],
        out_specs=(by_micro, by_kv),
        scratch_shapes=[pltpu.VMEM(held, F32)],
        compiler_params=params(),
        name="attend_backward",
    )(lens, place, queries, kv_all, attended, datt.reshape(micro, rows, QW), logsum)

    own_dkv = lax.psum_scatter(dkv, "fsdp", scatter_dimension=0, tiled=False)
    own_dkv = own_dkv.reshape(every, 2 * KW)

    if as_blocks:
        gattn = shape_of((count, deep, lanes), BF16)
    else:
        gattn = shape_of((width, QW + 2 * KW), F32)
    input_grad, grad_attn, grad_one = pl.pallas_call(
        functools.partial(post_kernel, members, as_blocks),
        grid=(micro,),
        out_shape=(shape_of((every, width), F32), gattn, shape_of((1, width), F32)),
        in_specs=[
            by_rows(width),
            by_rows(QW),
            by_rows(2 * KW),
            by_rows(width),
            same(width, QW + 2 * KW),
            same(1, width),
            by_rows(128),
            by_rows(128),
            same(QW, width),
            same(1, width),
        ],
        out_specs=(by_rows(width), same(*gattn.shape), same(1, width)),
        scratch_shapes=[
            pltpu.VMEM((every, QW + 2 * KW), BF16),
            pltpu.VMEM((every, width), BF16),
        ],
        compiler_params=params(),
        name="post",
    )(
        x,
        dq.reshape(every, QW),
        own_dkv,
        dmid,
        wqkv,
        gain_one,
        cosine,
        sine,
        grad_out,
        grad_two,
    )
    if not as_blocks:
        made = [None] * count

        def store(number, block):
            made[number] = block

        attention_blocks(grad_attn, grad_out, grad_one, grad_two, members, parts, store)
        grad_attn = jnp.stack(made)
    attn_sum = scatter_blocks(grad_attn)

    shapes = [
        (part, q_cols),
        (part, k_cols),
        (part, k_cols),
        w_out.shape,
        (1, part),
        (1, part),
        w_gate.shape,
        w_up.shape,
        w_down.shape,
    ]
    if as_blocks:
        grads = pl.pallas_call(
            unpack_kernel,
            out_shape=tuple(shape_of(s, F32) for s in shapes),
            in_specs=whole(2),
            out_specs=whole(9),
            compiler_params=params(),
            name="unpack",
        )(attn_sum, ffn_sum)
    else:
        grads = unpack_attention(attn_sum, part, q_cols, k_cols)
        grads += [ffn_sum[0].astype(F32), ffn_sum[1].astype(F32)]
        grads += [unpack_down(ffn_sum[2], w_down.shape)]
    return (
        mixed.reshape(tokens.shape),
        input_grad.reshape(tokens.shape),
        grads[4].reshape(-1),
        grads[0],
        grads[1],
        grads[2],
        grads[3],
        grads[5].reshape(-1),
        grads[6],
        grads[7],
        grads[8],
    )


def solution(mesh):
    rows = P(None, BOTH, None)
    block = P(*BOTH)
    gain = P("dp")
    in_specs = (rows, rows, P(None, "dp", None), gain)
    in_specs += (block, block, block, block, gain, block, block, block)
    out_specs = (rows, rows, gain, block, block, block, block, gain, block, block, block)
    return jax.shard_map(local, mesh=mesh, in_specs=in_specs, out_specs=out_specs, check_vma=False)
```

time: 1390 us -> 547 us (0.39)
  matrix products: 315 us -> 0 us
  blocking collectives: 282 us -> 0 us
  waiting for transfers between devices: 601 us -> 399 us
  other arithmetic: 113 us -> 3.48 us
  Pallas kernels: 0 us -> 107 us
  local copies, waits for them, and re-layouts: 46.1 us -> 22.1 us
    dot_general x135 -> x0, matrix products: 315 us -> none  [the longest x12 82.3 us: attend_backward(): jnp.einsum('tkrd,jkd->krtj', grad_attended, values_all[first_row:last_row...]
    all_gather x17 -> x0, blocking collectives: 217 us -> none  [the longest x1 33.2 us: fetch(): lax.all_gather(columns[0], 'dp', axis=0, tiled=True)]
    unnamed x38 -> x7, waiting for transfers between devices: 295 us -> 93 us
    reduce_scatter x5 -> x2, waiting for transfers between devices: 306 us -> 173 us  [the longest x1 103 us: scatter_blocks(): return lax.psum_scatter(blocks, BOTH, scatter_dimension=0, tiled=False)]
    all_gather x3, waiting for transfers between devices: 0.02 us -> 133 us  [the longest x2 106 us: gather_blocks(): return lax.all_gather(block, BOTH, axis=0, tiled=False)]
    pallas_call x0 -> x9, Pallas kernels: none -> 107 us  [the longest x1 42.3 us: local(): pl.pallas_call(functools.partial(mid_kernel, members, as_blocks), grid=(m...]
    unnamed x3 -> x0, blocking collectives: 64.8 us -> none
    convert_element_type x26 -> x1, other arithmetic: 64.5 us -> 0.01 us  [local(): posit = (at - begins).reshape(every, 1).astype(F32)]
  transfers between devices with their start and end apart: 23 -> 6, of which waited for: 18 -> 6; matrix products, arithmetic and copies ran while one was open for 25% -> 3% of each run, Pallas kernels for 0% -> 5%
where the time goes in v1:
time: 547 us; the launch traced here: 546 us
  waiting for transfers between devices  399 us (73%)
  Pallas kernels  107 us (20%)
  local copies, waits for them, and re-layouts  22.1 us (4%)
  between operations  14.2 us (3%)
    all_gather x2, waiting for transfers between devices, gather_blocks(): return lax.all_gather(block, BOTH, axis=0, tiled=False)  106 us
    reduce_scatter x1, waiting for transfers between devices, scatter_blocks(): return lax.psum_scatter(blocks, BOTH, scatter_dimension=0, tiled=False)  103 us
    unnamed x7, waiting for transfers between devices  93 us
    reduce_scatter x1, waiting for transfers between devices, local(): own_dkv = lax.psum_scatter(dkv, 'fsdp', scatter_dimension=0, tiled=False)  70.1 us
    pallas_call x1, Pallas kernels, local(): pl.pallas_call(functools.partial(mid_kernel, members, as_blocks), grid=(m...  42.3 us
    all_gather x1, waiting for transfers between devices, local(): kv_all = lax.all_gather(own_kv, 'fsdp', axis=0, tiled=False)  26.8 us
    unnamed x17, local copies, waits for them, and re-layouts  21.7 us
    pallas_call x1, Pallas kernels, local(): pl.pallas_call(backward_kernel, grid=(micro,), out_shape=(shape_of((micro...  19.4 us
  transfers between devices with their start and end apart: 6, of which 6 were waited for; matrix products, arithmetic and copies ran while one was open for 3% of the time, Pallas kernels for 5%

profile of v1, /device:TPU:0, one launch (start us, length us, event | category | flops | bytes accessed | tf_op | source)
XLA Modules:
  0.0 545.9 jit_solution(4305739537017610175)
XLA Ops:
  7.2 1.4 copy.44.k
  8.6 1.4 copy.45.v
  10.0 1.6 copy.46.down
  11.7 1.9 pack.1
  13.7 0.7 copy.55
  14.4 0.2 reduce_window_sum.11
  14.5 0.2 slice_reduce_fusion
  14.7 0.1 le.60
  15.0 3.5 copy.43
  18.5 3.3 fusion
  21.8 50.8 %all-gather.7.cloned.1.call-done = bf16[2560,384]{1,0:T(8,128)(2,1)} async-done(((bf16[80,384]{1,0:T(8,128)(2,1)}), bf16[2560,384]{1,0:T(8,128)(2,1)}) %all-gather.7.cloned.1.call-update) | async-done | bytes 1966096 | tf_op jit(solution)/shard_map/all_gather | solution.py:520
  72.6 3.8 join_attention.1
  76.4 6.5 %pre.1 = (bf16[1152,576]{1,0:T(8,128)(2,1)}, bf16[1152,384]{1,0:T(8,128)(2,1)}) custom-call(bf16[1152,576]{1,0:T(8,128)(2,1)} %bitcast.22, bf16[576,960]{1,0:T(8,128)(2,1)} %get-tuple-element.44.w_ref, f32[1,576]{1,0:T(1,128)} %get-tuple-element.45.gain_ref, f32[1152,128]{1,0:T(8,128)} %get-tuple-element.112.cos_ref, f32[1152,128]{1,0:T(8,128)} %get-tuple-element.111.sin_ref), custom_call_target="tpu_custom_call" | custom-call | tf_op jit(solution)/shard_map/pre/pallas_call | solution.py:622
  83.0 0.7 all-gather.11.cloned.1.call-update
  83.8 2.1 copy.47
  85.9 26.8 %all-gather.9.cloned.1.call-done = bf16[4608,384]{1,0:T(8,128)(2,1)} async-done(((bf16[1152,384]{1,0:T(8,128)(2,1)}), bf16[4608,384]{1,0:T(8,128)(2,1)}) %all-gather.9.cloned.1.call-update) | async-done | bytes 3538960 | tf_op jit(solution)/shard_map/all_gather | solution.py:638
  112.7 13.6 %attend_forward.1 = (f32[3,384,576]{2,1,0:T(8,128)}, f32[3,3,1,1152]{3,2,1,0:T(1,128)}) custom-call(s32[3,3]{1,0:T(4,128)} %bitcast.41, s32[1]{0:T(128)} %bitcast.1.place_ref, bf16[3,384,576]{2,1,0:T(8,128)(2,1)} %bitcast.28, bf16[4,3,384,384]{3,2,1,0:T(8,128)(2,1)} %bitcast.25), custom_call_target="tpu_custom_call" | custom-call | tf_op jit(solution)/shard_map/attend_forward/pallas_call | solution.py:648
  126.3 54.9 %all-gather.11.cloned.1.call-done = bf16[96,72,384]{2,1,0:T(8,128)(2,1)} async-done(((bf16[3,72,384]{2,1,0:T(8,128)(2,1)}), bf16[96,72,384]{2,1,0:T(8,128)(2,1)}) %all-gather.11.cloned.1.call-update) | async-done | bytes 5308432 | tf_op jit(solution)/shard_map/all_gather | solution.py:520
  181.2 5.4 join_ffn.1
  186.6 42.3 %mid.1 = (bf16[1152,576]{1,0:T(8,128)(2,1)}, f32[1152,576]{1,0:T(8,128)}, bf16[1152,576]{1,0:T(8,128)(2,1)}, f32[576,576]{1,0:T(8,128)}, bf16[32,3,72,384]{3,2,1,0:T(8,128)(2,1)}, /*index=5*/f32[1,576]{1,0:T(1,128)}) custom-call(bf16[1152,576]{1,0:T(8,128)(2,1)} %bitcast.23, f32[1152,576]{1,0:T(8,128)} %bitcast.27, bf16[1152,576]{1,0:T(8,128)(2,1)} %bitcast.30, ...), custom_call_target="tpu_custom_call" | custom-call | tf_op jit(solution)/shard_map/mid/pallas_call | solution.py:663
  229.0 19.4 %attend_backward.1 = (f32[3,384,576]{2,1,0:T(8,128)}, bf16[4,3,384,384]{3,2,1,0:T(8,128)(2,1)}) custom-call(s32[3,3]{1,0:T(4,128)} %bitcast.42, s32[1]{0:T(128)} %bitcast.1.place_ref, bf16[3,384,576]{2,1,0:T(8,128)(2,1)} %bitcast.29, bf16[4,3,384,384]{3,2,1,0:T(8,128)(2,1)} %bitcast.26, f32[3,384,576]{2,1,0:T(8,128)} %get-tuple-element.48.out_ref, ...), custom_call_target="tpu_custom_call" | custom-call | tf_op jit(solution)/shard_map/attend_backward/pallas_call | solution.py:709
  248.5 0.5 reduce-scatter.10.cloned.1.call-update
  249.1 70.1 %reduce-scatter.6.cloned.1.call-done = bf16[1,3,384,384]{3,2,1,0:T(8,128)(2,1)} async-done(((bf16[4,3,384,384]{3,2,1,0:T(8,128)(2,1)}), bf16[1,3,384,384]{3,2,1,0:T(8,128)(2,1)}) %reduce-scatter.6.cloned.1.call-update) | async-done | bytes 884752 | tf_op jit(solution)/shard_map/reduce_scatter | solution.py:723
  319.2 12.4 %post.1 = (f32[1152,576]{1,0:T(8,128)}, bf16[32,80,384]{2,1,0:T(8,128)(2,1)}, f32[1,576]{1,0:T(1,128)}) custom-call(bf16[1152,576]{1,0:T(8,128)(2,1)} %bitcast.24, f32[1152,576]{1,0:T(8,128)} %bitcast.32, bf16[1152,384]{1,0:T(8,128)(2,1)} %bitcast.37, f32[1152,576]{1,0:T(8,128)} %get-tuple-element.60.dmid_ref, bf16[576,960]{1,0:T(8,128)(2,1)} %get-tuple-element.44.w_ref, ...), custom_call_target="tpu_custom_call" | custom-call | tf_op jit(solution)/shard_map/post/pallas_call | solution.py:730
  331.6 3.7 copy.48
  335.3 2.6 copy.49
  337.9 91.8 %reduce-scatter.10.cloned.1.call-done = bf16[1,3,72,384]{3,2,1,0:T(8,128)(2,1)} async-done(((bf16[32,3,72,384]{3,2,1,0:T(8,128)(2,1)}), bf16[1,3,72,384]{3,2,1,0:T(8,128)(2,1)}) %reduce-scatter.10.cloned.1.call-update) | async-done | bytes 165904
  429.7 102.9 %reduce-scatter.8.cloned.1.call-done = bf16[1,80,384]{2,1,0:T(8,128)(2,1)} async-done(((bf16[32,80,384]{2,1,0:T(8,128)(2,1)}), bf16[1,80,384]{2,1,0:T(8,128)(2,1)}) %reduce-scatter.8.cloned.1.call-update) | async-done | bytes 61456 | tf_op jit(solution)/shard_map/reduce_scatter | solution.py:524
  532.6 1.9 unpack.1
  534.4 1.5 copy.50
  535.9 1.5 copy.51
  537.3 1.7 copy.52
  (26 shorter events, 0.5 us)
Async XLA Ops:
  7.2 65.4 %all-gather.7.cloned.1.call-start = ((), (), s32[]{:S(2)}) async-start(), calls=%async_computation.5 | async-start | bytes 2027520 | tf_op jit(solution)/shard_map/all_gather | solution.py:520
  13.6 99.1 %all-gather.9.cloned.1.call-start = ((), (), s32[]{:S(2)}) async-start(), calls=%async_computation.6 | async-start | bytes 4423680 | tf_op jit(solution)/shard_map/all_gather | solution.py:638
  14.3 7.5 %copy-start.2 = (s32[3,1,3]{2,0,1:T(4,128)}, s32[3,1,3]{2,0,1:T(4,128)S(1)}, u32[]{:S(2)}) copy-start(s32[3,1,3]{2,0,1:T(4,128)S(1)} %copy.55) | copy-start | bytes 112
  76.4 7.3 %copy-start.1 = (bf16[3,384,576]{1,2,0:T(8,128)(2,1)S(1)}, bf16[3,384,576]{1,2,0:T(8,128)(2,1)}, u32[]{:S(2)}) copy-start(bf16[3,384,576]{1,2,0:T(8,128)(2,1)} %param.13) | copy-start | bytes 3981316
  83.0 98.3 %all-gather.11.cloned.1.call-start = ((), (), s32[]{:S(2)}) async-start(), calls=%async_computation.7 | async-start | bytes 5474304 | tf_op jit(solution)/shard_map/all_gather | solution.py:520
  83.7 235.4 %reduce-scatter.6.cloned.1.call-start = ((), (), s32[]{:S(2)}) async-start(), calls=%async_computation.3 | async-start | bytes 4423680 | tf_op jit(solution)/shard_map/reduce_scatter | solution.py:723
  248.4 181.3 %reduce-scatter.10.cloned.1.call-start = ((), (), s32[]{:S(2)}) async-start(), calls=%async_computation.8 | async-start | bytes 5474304
  249.0 283.6 %reduce-scatter.8.cloned.1.call-start = ((), (), s32[]{:S(2)}) async-start(), calls=%async_computation.4 | async-start | bytes 2027520 | tf_op jit(solution)/shard_map/reduce_scatter | solution.py:524
  331.6 3.8 copy-start
Sparse Core Ops, SparseCore 0:
  13.7 58.8 all-gather.6
  83.1 29.5 all-gather.8
  115.6 65.6 all-gather.10
  248.6 70.5 reduce-scatter.5
  325.7 103.9 reduce-scatter.9
  435.6 96.9 reduce-scatter.7
